TPU v7x, 512 devices: a whole 4x4x16 slice. The times are simulated.
512 devices in a mesh: env: 64 (over x, z_lo, core), row: 8 (over y, z_hi).
Axes of the slice: x: 4, y: 4, z: 16 (z_hi: 2, z_lo: 8; z = z_hi * 8 + z_lo), core: 2. Of those that a mesh axis runs over, the one named last changes fastest.
Arguments:
- descriptors: bfloat16 [131072, 1024], P(('env', 'row')), may hold values from -6 to 6
- directions: bfloat16 [64, 131072], P(None, ('env', 'row')), may hold values from -6 to 6
- ridge: float32 [64], replicated, may hold values from 0.5 to 2
- partner: int32 [2, 64], replicated, may hold values from 0 to 63, as said below
Outputs:
- image: float32 [64, 131072], P(None, ('env', 'row'))
Inputs may be any that keep to these rules, and one draw needn't show every extreme that they name: For each round r there is a mask m_r, 1 to 63, the same for all blocks, with partner[r, b] = b XOR m_r; the masks of different rounds differ.
All inputs are finite; a program needn't handle non-finite values.
Results may differ from a plain program's by a relative error of at most 0.0029.
Values may be sent and summed in bfloat16 or wider, within the bound.
No kernel may reach another device: no remote copies, remote signals or barrier semaphores. Data moves between devices by JAX's collectives and lax.ppermute only.
A program may use at most 64 MiB of HBM per device.

v0:
```python
import jax
import jax.numpy as jnp
from jax import lax
from jax.experimental import pallas as pl
from jax.experimental.pallas import tpu as pltpu
from jax.sharding import PartitionSpec as P

DESC = 1024
ROUNDS = 2
AXES = ("env", "row")
ENV = 64
ROW = 8
GROUP = 4
SIDE = 8
STEPS = 10


def parity(value):
    return bin(value).count("1") & 1


def far_step(step):
    if step < 7:
        low = step + 1
        top = low.bit_length() - 1
        for bits in range(1, 8):
            if parity(bits & low) and bits != 1 << top:
                return low << 1, bits << 1
    return 0, {0: 1, 1: 16, 2: 32}[(step - 7) % 3]


def far_pairs(step):
    mask, bits = far_step(step)
    pairs = []
    for env in range(ENV):
        target = env ^ mask
        for row in range(ROW):
            pairs.append((env * ROW + row, target * ROW + (row ^ parity(target & bits))))
    return pairs


def back_pairs(step):
    if step < STEPS:
        return [(target, source) for source, target in far_pairs(step)]
    mask, bits = far_step(step)
    return [
        (env * ROW + row, env * ROW + (row ^ 1 ^ parity(env & bits)))
        for env in range(ENV)
        for row in range(ROW)
    ]


def side_pairs(side):
    mask = (side >> 1) << 4 | (side & 1)
    return [(e * ROW + r, (e ^ mask) * ROW + r) for e in range(ENV) for r in range(ROW)]


def near_groups():
    return [[2 * y + half for y in range(GROUP)] for half in range(2)]


def side_groups():
    return [[(p >> 1) << 4 | z << 1 | (p & 1) for p in range(SIDE)] for z in range(8)]


def moved(value, pairs):
    return lax.ppermute(value, AXES, pairs)


def beside(value, side):
    return moved(value, side_pairs(side)) if side else value


def start_kernel(partner, desc, dirs, packed, copies, far0, side0, far1, side1, back0, sem):
    rows = desc.shape[0]
    copy = pltpu.make_async_copy(desc, packed.at[0:rows], sem.at[0])
    copy.start()
    for r, (far, side) in enumerate(((far0, side0), (far1, side1))):
        mask = partner[r, 0]
        low = (mask >> 1) & 7
        other = jnp.where((mask & 1) == 1, 7, jnp.where((mask & 16) == 16, 8, 9))
        far[0, 0] = jnp.where(low > 0, low - 1, other)
        side[0, 0] = ((mask >> 4) << 1) | (mask & 1)
    back0[0, 0] = far0[0, 0] + jnp.where(far0[0, 0] < 7, 0, 3)
    for j in range(4):
        packed[rows : rows + 16, j * rows : (j + 1) * rows] = dirs[16 * j : 16 * j + 16, :]
    copy.wait()
    spread = [pltpu.make_async_copy(packed, copies.at[k], sem.at[1 + k]) for k in range(GROUP)]
    for copy in spread:
        copy.start()
    for copy in spread:
        copy.wait()


def start(partner, desc, dirs):
    index = jax.ShapeDtypeStruct((1, 1), jnp.int32)
    smem = pl.BlockSpec(memory_space=pltpu.SMEM)
    vmem = pl.BlockSpec(memory_space=pltpu.VMEM)
    packed, copies, *steps = pl.pallas_call(
        start_kernel,
        out_shape=(
            jax.ShapeDtypeStruct((desc.shape[0] + 16, DESC), desc.dtype),
            jax.ShapeDtypeStruct((GROUP, desc.shape[0] + 16, DESC), desc.dtype),
        )
        + (index,) * 5,
        in_specs=[smem, pl.BlockSpec(memory_space=pl.ANY), vmem],
        out_specs=(vmem, pl.BlockSpec(memory_space=pl.ANY)) + (smem,) * 5,
        scratch_shapes=[pltpu.SemaphoreType.DMA((1 + GROUP,))],
    )(partner, desc, dirs)
    return packed, copies, [step.reshape(()) for step in steps]


def dot(left, right, left_dim, right_dim):
    return lax.dot_general(
        left, right, (((left_dim,), (right_dim,)), ((), ())), preferred_element_type=jnp.float32
    )


def unpacked(flat, rows):
    return jnp.concatenate([flat[:, j * rows : (j + 1) * rows] for j in range(4)], axis=0)


def tiles_kernel(first, second, group, to_far, to_near, far, flat, held, sems):
    rhs, rows = to_far.shape[1:]
    copies = [
        pltpu.make_async_copy(first.at[0:rows], far.at[0:rows], sems.at[0]),
        pltpu.make_async_copy(second.at[0:rows], far.at[rows : 2 * rows], sems.at[1]),
        pltpu.make_async_copy(first.at[rows : rows + 16], flat.at[0], sems.at[2]),
        pltpu.make_async_copy(second.at[rows : rows + 16], flat.at[1], sems.at[3]),
    ]
    copies += [pltpu.make_async_copy(group.at[k], held.at[k], sems.at[4 + k]) for k in range(GROUP)]
    for copy in copies:
        copy.start()
    for copy in copies[:4]:
        copy.wait()
    far_dirs = jnp.concatenate([unpacked(flat[r], rows) for r in range(ROUNDS)], axis=1)
    total = jnp.zeros((rhs, 2 * rows), jnp.float32)
    for k in range(GROUP):
        copies[4 + k].wait()
        gram = dot(held[k, 0:rows, :], far[...], 1, 1)
        shifted = 1.0 + gram * DESC ** (-0.5)
        tile = (shifted * shifted).astype(jnp.bfloat16)
        total = total + dot(unpacked(held[k, rows : rows + 16, :], rows), tile, 1, 0)
        to_near[k] = dot(far_dirs, tile, 1, 1)
    to_far[0] = total[:, 0:rows].astype(to_far.dtype)
    to_far[1] = total[:, rows:].astype(to_far.dtype)


def tiles(group, first, second, rhs):
    rows = first.shape[0] - 16
    vmem = pl.BlockSpec(memory_space=pltpu.VMEM)
    hbm = pl.BlockSpec(memory_space=pl.ANY)
    return pl.pallas_call(
        tiles_kernel,
        out_shape=(
            jax.ShapeDtypeStruct((ROUNDS, rhs, rows), jnp.bfloat16),
            jax.ShapeDtypeStruct((GROUP, rhs, rows), jnp.float32),
        ),
        in_specs=[hbm] * 3,
        out_specs=(vmem, vmem),
        scratch_shapes=[
            pltpu.VMEM((2 * rows, DESC), jnp.bfloat16),
            pltpu.VMEM((ROUNDS, 16, DESC), jnp.bfloat16),
            pltpu.VMEM(group.shape, jnp.bfloat16),
            pltpu.SemaphoreType.DMA((4 + GROUP,)),
        ],
        compiler_params=pltpu.CompilerParams(vmem_limit_bytes=24 * 1024 * 1024),
        cost_estimate=pl.CostEstimate(
            flops=16 * rows * rows * (DESC + 2 * rhs),
            bytes_accessed=6 * rows * DESC * 2,
            transcendentals=0,
        ),
    )(first, second, group)


def pick(index, count, branch_of, *operands):
    return lax.switch(index, [branch_of(i) for i in range(count)], *operands)


def side_step(side, value):
    return pick(side, SIDE, lambda s: lambda v: beside(v, s), value)


def exchanged(value, axis, groups):
    return lax.all_to_all(value, axis, 0, 0, axis_index_groups=groups)


def on_device(descriptors, directions, ridge, partner):
    rhs, rows = directions.shape
    weight = (ROUNDS * rows * ROW) ** (-0.5)
    packed, copies, (far0, side0, far1, side1, back0) = start(partner, descriptors, directions)

    def out_first(far):
        def branch(value, side):
            return side_step(side, value), moved(value, far_pairs(far))

        return branch

    def out_second(far):
        def branch(first, second, copies, side):
            group = exchanged(copies, "row", near_groups())
            return group, side_step(side, first), moved(second, far_pairs(far))

        return branch

    def back_both(far):
        def branch(first, second, other_far):
            first = pick(
                other_far, STEPS + 3, lambda f: lambda v: moved(v, back_pairs(f)), first
            )
            return first, moved(second, back_pairs(far))

        return branch

    second, first = pick(far0, STEPS, out_first, packed, side1)
    group, first, second = pick(far1, STEPS, out_second, first, second, copies, side0)
    to_far, to_near = tiles(group, first, second, rhs)
    near = exchanged(to_near, "row", near_groups())
    first, second = pick(far1, STEPS, back_both, to_far[0], to_far[1], back0)
    env = lax.axis_index("env")
    place = (env >> 4) << 1 | (env & 1)
    slots = jnp.arange(SIDE, dtype=jnp.int32)[:, None, None]
    none = jnp.zeros_like(first)
    sent = jnp.where(slots == place ^ side0, first, none)
    sent = sent + jnp.where(slots == place ^ side1, second, none)
    side = exchanged(sent, "env", side_groups())
    result = jnp.sum(near, axis=0) + jnp.sum(side.astype(jnp.float32), axis=0)
    return ridge[:, None] * directions.astype(jnp.float32) + weight * result


def solution(mesh):
    return jax.shard_map(
        on_device,
        mesh=mesh,
        in_specs=(P(("env", "row"), None), P(None, ("env", "row")), P(), P()),
        out_specs=P(None, ("env", "row")),
        check_vma=False,
    )
```

profile of v0, /device:TPU:1, one launch (start us, length us, event | category | flops | bytes accessed | tf_op | source)
XLA Modules:
  0.0 136.3 jit_solution(3592931285532710287)
XLA Ops:
  0.0 4.1 %shard_map.46 = (bf16[272,1024]{1,0:T(8,128)(2,1)}, bf16[4,272,1024]{2,1,0:T(8,128)(2,1)}, s32[1,1]{1,0:T(1,128)}, s32[1,1]{1,0:T(1,128)}, s32[1,1]{1,0:T(1,128)}, /*index=5*/s32[1,1]{1,0:T(1,128)}, s32[1,1]{1,0:T(1,128)}) custom-call(s32[2,64]{1,0:T(2,128)} %partner.1, bf16[256,1024]{1,0:T(8,128)(2,1)} %desc.1, bf16[64,256]{1,0:T(8,128)(2,1)} %dirs.1), custom_call_target="tpu_custom_call" | custom-call | tf_op jit(solution)/shard_map/pallas_call | solution.py:99
  5.3 30.7 %conditional.33 = (bf16[272,1024]{1,0:T(8,128)(2,1)}, bf16[272,1024]{1,0:T(8,128)(2,1)}) conditional(s32[]{:T(128)} %bitcast.2, (s32[]{:T(128)}, bf16[272,1024]{1,0:T(8,128)(2,1)}) %tuple.995, (s32[]{:T(128)}, bf16[272,1024]{1,0:T(8,128)(2,1)}) %tuple.995, (s32[]{:T(128)}, bf16[272,1024]{1,0:T(8,128)(2,1)}) %tuple.995, ...), branch_computations={%region_0.0_spmd, %region_9.0_spmd, %region_18.0_spmd, %region_27.... | conditional | flops 1 | bytes 4456568 | solution.py:177
  5.4 14.9 %collective-permute-start.23 = (bf16[272,1024]{1,0:T(8,128)(2,1)}, bf16[272,1024]{1,0:T(8,128)(2,1)}, u32[]{:S(2)}, u32[]{:S(2)}) collective-permute-start(bf16[272,1024]{1,0:T(8,128)(2,1)} %get-tuple-element.800), channel_id=1, source_target_pairs={{0,49},{1,48},{2,51},{3,50},{4,53},{5,52},{6,55},{7,54},{8,57},{9,... | collective-permute-start | bytes 1671176 | tf_op jit(solution)/shard_map/cond/branch_2_fun/ppermute | solution.py:67
  21.0 1.9 %conditional.2 = (bf16[272,1024]{1,0:T(8,128)(2,1)}) conditional(s32[]{:T(128)} %clamp.71, bf16[272,1024]{1,0:T(8,128)(2,1)} %get-tuple-element.800, bf16[272,1024]{1,0:T(8,128)(2,1)} %get-tuple-element.800, bf16[272,1024]{1,0:T(8,128)(2,1)} %get-tuple-element.800, bf16[272,1024]{1,0:T(8,128)(2,1)} %get-tuple-element.800, ...), branch_computations={%region_19.0_spmd, %region_20.0_spmd, %region_21.0_spmd, %region_2... | conditional | bytes 2228272 | solution.py:177
  21.0 1.9 %copy.21 = bf16[272,1024]{1,0:T(8,128)(2,1)} copy(bf16[272,1024]{1,0:T(8,128)(2,1)} %param.18) | data formatting | bytes 1114112 | tf_op jit(solution)/shard_map/cond/branch_2_fun/cond
  22.9 13.1 %collective-permute-done.23 = bf16[272,1024]{1,0:T(8,128)(2,1)} collective-permute-done((bf16[272,1024]{1,0:T(8,128)(2,1)}, bf16[272,1024]{1,0:T(8,128)(2,1)}, u32[]{:S(2)}, u32[]{:S(2)}) %collective-permute-start.23) | collective-permute-done | bytes 557088 | tf_op jit(solution)/shard_map/cond/branch_2_fun/ppermute | solution.py:67
  36.0 46.1 %conditional.34 = (bf16[4,272,1024]{2,1,0:T(8,128)(2,1)}, bf16[272,1024]{1,0:T(8,128)(2,1)}, bf16[272,1024]{1,0:T(8,128)(2,1)}) conditional(s32[]{:T(128)} %bitcast, (bf16[4,272,1024]{2,1,0:T(8,128)(2,1)}, s32[]{:T(128)}, bf16[272,1024]{1,0:T(8,128)(2,1)}, bf16[272,1024]{1,0:T(8,128)(2,1)}) %tuple.996, ...), branch_computations={%region_90.0_spmd, %region_99.0_spmd, %region_108.0_spmd, %region_... | conditional | flops 1 | bytes 12255392 | solution.py:177
  36.0 4.5 %all-to-all-start.4 = ((bf16[4,272,1024]{2,1,0:T(8,128)(2,1)}), bf16[4,272,1024]{2,1,0:T(8,128)(2,1)}, u32[]{:S(2)}, u32[]{:S(2)}) async-start(bf16[4,272,1024]{2,1,0:T(8,128)(2,1)} %get-tuple-element.831), calls=%async_computation.4 | async-start | bytes 4456448 | tf_op jit(solution)/shard_map/cond/branch_4_fun/all_to_all | solution.py:185
  40.6 17.6 %collective-permute-start.119 = (bf16[272,1024]{1,0:T(8,128)(2,1)}, bf16[272,1024]{1,0:T(8,128)(2,1)}, u32[]{:S(2)}, u32[]{:S(2)}) collective-permute-start(bf16[272,1024]{1,0:T(8,128)(2,1)} %get-tuple-element.834), channel_id=1, source_target_pairs={{0,81},{1,80},{2,83},{3,82},{4,85},{5,84},{6,87},{7,86},{8,89},{9,... | collective-permute-start | bytes 1671176 | tf_op jit(solution)/shard_map/cond/branch_4_fun/ppermute | solution.py:67
  58.8 14.5 %conditional.14 = (bf16[272,1024]{1,0:T(8,128)(2,1)}) conditional(s32[]{:T(128)} %clamp.83, bf16[272,1024]{1,0:T(8,128)(2,1)} %get-tuple-element.833, bf16[272,1024]{1,0:T(8,128)(2,1)} %get-tuple-element.833, bf16[272,1024]{1,0:T(8,128)(2,1)} %get-tuple-element.833, ...), branch_computations={%region_127.0_spmd, %region_128.0_spmd, %region_129.0_spmd, %regio... | conditional | bytes 2228272 | solution.py:177
  58.9 3.1 %collective-permute-start.113 = (bf16[272,1024]{1,0:T(8,128)(2,1)}, bf16[272,1024]{1,0:T(8,128)(2,1)}, u32[]{:S(2)}, u32[]{:S(2)}) collective-permute-start(bf16[272,1024]{1,0:T(8,128)(2,1)} %param.128), channel_id=1, source_target_pairs={{0,128},{1,129},{2,130},{3,131},{4,132},{5,133},{6,134},{7,135},{8... | collective-permute-start | bytes 1671176 | tf_op jit(solution)/shard_map/cond/branch_4_fun/cond/branch_2_fun/ppermute | solution.py:67
  62.0 11.3 %collective-permute-done.113 = bf16[272,1024]{1,0:T(8,128)(2,1)} collective-permute-done((bf16[272,1024]{1,0:T(8,128)(2,1)}, bf16[272,1024]{1,0:T(8,128)(2,1)}, u32[]{:S(2)}, u32[]{:S(2)}) %collective-permute-start.113) | collective-permute-done | bytes 557088 | tf_op jit(solution)/shard_map/cond/branch_4_fun/cond/branch_2_fun/ppermute | solution.py:67
  73.3 1.9 %copy.328 = bf16[272,1024]{1,0:T(8,128)(2,1)} copy(bf16[272,1024]{1,0:T(8,128)(2,1)} %get-tuple-element.1005) | data formatting | bytes 1114112 | tf_op jit(solution)/shard_map/cond
  75.2 6.9 %collective-permute-done.119 = bf16[272,1024]{1,0:T(8,128)(2,1)} collective-permute-done((bf16[272,1024]{1,0:T(8,128)(2,1)}, bf16[272,1024]{1,0:T(8,128)(2,1)}, u32[]{:S(2)}, u32[]{:S(2)}) %collective-permute-start.119) | collective-permute-done | bytes 557088 | tf_op jit(solution)/shard_map/cond/branch_4_fun/ppermute | solution.py:67
  82.1 0.0 all-to-all-done.4
  82.2 5.0 %shard_map.47 = (bf16[2,64,256]{2,1,0:T(8,128)(2,1)S(1)}, f32[4,64,256]{2,1,0:T(8,128)}) custom-call(bf16[272,1024]{1,0:T(8,128)(2,1)} %get-tuple-element.909.first, bf16[272,1024]{1,0:T(8,128)(2,1)} %get-tuple-element.910.second, bf16[4,272,1024]{2,1,0:T(8,128)(2,1)} %get-tuple-element.911.group), custom_call_target="tpu_custom_call" | custom-call | flops 1207959552 | bytes 3145728 | tf_op jit(solution)/shard_map/pallas_call | solution.py:153
  87.1 0.0 copy-start
  87.1 0.0 copy-start.1
  87.1 4.2 %all-to-all-start.10 = ((f32[4,64,256]{2,1,0:T(8,128)}), f32[4,64,256]{2,1,0:T(8,128)S(1)}, u32[]{:S(2)}, u32[]{:S(2)}) async-start(f32[4,64,256]{2,1,0:T(8,128)} %get-tuple-element.912), calls=%async_computation.10 | async-start | bytes 524288 | tf_op jit(solution)/shard_map/all_to_all | solution.py:185
  92.7 29.3 %conditional.35 = (bf16[64,256]{1,0:T(8,128)(2,1)}, bf16[64,256]{1,0:T(8,128)(2,1)}) conditional(s32[]{:T(128)} %bitcast, (s32[]{:T(128)}, bf16[64,256]{1,0:T(8,128)(2,1)S(1)}, bf16[64,256]{1,0:T(8,128)(2,1)S(1)}) %tuple.997, (s32[]{:T(128)}, bf16[64,256]{1,0:T(8,128)(2,1)S(1)}, ...), branch_computations={%region_181.195_spmd, %region_195.209_spmd, %region_209.223_spmd, ... | conditional | flops 1 | bytes 262264 | solution.py:177
  92.7 14.6 %collective-permute-start.229 = (bf16[64,256]{1,0:T(8,128)(2,1)S(1)}, bf16[64,256]{1,0:T(8,128)(2,1)}, u32[]{:S(2)}, u32[]{:S(2)}) collective-permute-start(bf16[64,256]{1,0:T(8,128)(2,1)S(1)} %get-tuple-element.869), channel_id=1, source_target_pairs={{81,0},{80,1},{83,2},{82,3},{85,4},{84,5},{87,6},{86,7},{89,8},{88... | collective-permute-start | bytes 98312 | tf_op jit(solution)/shard_map/cond/branch_4_fun/ppermute | solution.py:67
  108.0 14.0 %conditional.24 = (bf16[64,256]{1,0:T(8,128)(2,1)}) conditional(s32[]{:T(128)} %clamp.93, bf16[64,256]{1,0:T(8,128)(2,1)S(1)} %get-tuple-element.868, bf16[64,256]{1,0:T(8,128)(2,1)S(1)} %get-tuple-element.868, bf16[64,256]{1,0:T(8,128)(2,1)S(1)} %get-tuple-element.868, ...), branch_computations={%region_238.0_spmd, %region_239.0_spmd, %region_240.0_spmd, %regio... | conditional | bytes 131120 | solution.py:177
  108.0 5.8 %collective-permute-start.218 = (bf16[64,256]{1,0:T(8,128)(2,1)S(1)}, bf16[64,256]{1,0:T(8,128)(2,1)}, u32[]{:S(2)}, u32[]{:S(2)}) collective-permute-start(bf16[64,256]{1,0:T(8,128)(2,1)S(1)} %param.238), channel_id=1, source_target_pairs={{49,0},{48,1},{51,2},{50,3},{53,4},{52,5},{55,6},{54,7},{57,8},{56... | collective-permute-start | bytes 98312 | tf_op jit(solution)/shard_map/cond/branch_4_fun/cond/branch_2_fun/ppermute | solution.py:67
  113.8 8.2 %collective-permute-done.218 = bf16[64,256]{1,0:T(8,128)(2,1)} collective-permute-done((bf16[64,256]{1,0:T(8,128)(2,1)S(1)}, bf16[64,256]{1,0:T(8,128)(2,1)}, u32[]{:S(2)}, u32[]{:S(2)}) %collective-permute-start.218) | collective-permute-done | bytes 32800 | tf_op jit(solution)/shard_map/cond/branch_4_fun/cond/branch_2_fun/ppermute | solution.py:67
  122.0 0.0 collective-permute-done.229
  122.0 1.6 %select_add_fusion = bf16[8,64,256]{2,1,0:T(8,128)(2,1)} fusion(pred[8]{0:T(512)(128)(4,1)S(1)} %get-tuple-element.919, pred[8]{0:T(512)(128)(4,1)S(1)} %get-tuple-element.920, bf16[64,256]{1,0:T(8,128)(2,1)} %get-tuple-element.916, bf16[64,256]{1,0:T(8,128)(2,1)} %get-tuple-element.915), kind=kLoop, calls=%fused_computation.1 | loop fusion | flops 393216 | bytes 327696 | tf_op jit(solution)/shard_map/add | solution.py:225
  123.6 0.0 all-to-all-done.10
  123.6 5.5 %all-to-all-start.11 = ((bf16[8,64,256]{2,1,0:T(8,128)(2,1)}), bf16[8,64,256]{2,1,0:T(8,128)(2,1)S(1)}, u32[]{:S(2)}, u32[]{:S(2)}) async-start(bf16[8,64,256]{2,1,0:T(8,128)(2,1)} %select_add_fusion), calls=%async_computation.11 | async-start | bytes 524288 | tf_op jit(solution)/shard_map/all_to_all | solution.py:185
  129.1 6.5 %all-to-all-done.11 = bf16[8,64,256]{2,1,0:T(8,128)(2,1)S(1)} async-done(((bf16[8,64,256]{2,1,0:T(8,128)(2,1)}), bf16[8,64,256]{2,1,0:T(8,128)(2,1)S(1)}, u32[]{:S(2)}, u32[]{:S(2)}) %all-to-all-start.11) | async-done | bytes 262176 | tf_op jit(solution)/shard_map/all_to_all | solution.py:185
  135.6 0.0 copy-done
  135.6 0.0 copy-done.1
  135.6 0.7 multiply_add_fusion
  (4 shorter events, 0.1 us)
Async XLA Ops:
  5.4 30.7 %collective-permute-start.23 = (bf16[272,1024]{1,0:T(8,128)(2,1)}, bf16[272,1024]{1,0:T(8,128)(2,1)}, u32[]{:S(2)}, u32[]{:S(2)}) collective-permute-start(bf16[272,1024]{1,0:T(8,128)(2,1)} %get-tuple-element.800), channel_id=1, source_target_pairs={{0,49},{1,48},{2,51},{3,50},{4,53},{5,52},{6,55},{7,54},{8,57},{9,... | collective-permute-start | bytes 1671176 | tf_op jit(solution)/shard_map/cond/branch_2_fun/ppermute | solution.py:67
  36.0 46.1 %all-to-all-start.4 = ((bf16[4,272,1024]{2,1,0:T(8,128)(2,1)}), bf16[4,272,1024]{2,1,0:T(8,128)(2,1)}, u32[]{:S(2)}, u32[]{:S(2)}) async-start(bf16[4,272,1024]{2,1,0:T(8,128)(2,1)} %get-tuple-element.831), calls=%async_computation.4 | async-start | bytes 4456448 | tf_op jit(solution)/shard_map/cond/branch_4_fun/all_to_all | solution.py:185
  40.6 41.6 %collective-permute-start.119 = (bf16[272,1024]{1,0:T(8,128)(2,1)}, bf16[272,1024]{1,0:T(8,128)(2,1)}, u32[]{:S(2)}, u32[]{:S(2)}) collective-permute-start(bf16[272,1024]{1,0:T(8,128)(2,1)} %get-tuple-element.834), channel_id=1, source_target_pairs={{0,81},{1,80},{2,83},{3,82},{4,85},{5,84},{6,87},{7,86},{8,89},{9,... | collective-permute-start | bytes 1671176 | tf_op jit(solution)/shard_map/cond/branch_4_fun/ppermute | solution.py:67
  58.9 14.5 %collective-permute-start.113 = (bf16[272,1024]{1,0:T(8,128)(2,1)}, bf16[272,1024]{1,0:T(8,128)(2,1)}, u32[]{:S(2)}, u32[]{:S(2)}) collective-permute-start(bf16[272,1024]{1,0:T(8,128)(2,1)} %param.128), channel_id=1, source_target_pairs={{0,128},{1,129},{2,130},{3,131},{4,132},{5,133},{6,134},{7,135},{8... | collective-permute-start | bytes 1671176 | tf_op jit(solution)/shard_map/cond/branch_4_fun/cond/branch_2_fun/ppermute | solution.py:67
  87.1 48.5 %copy-start = (bf16[64,256]{1,0:T(8,128)(2,1)S(1)}, bf16[64,256]{1,0:T(8,128)(2,1)}, u32[]{:S(2)}) copy-start(bf16[64,256]{1,0:T(8,128)(2,1)} %dirs.1) | copy-start | bytes 98308
  87.1 48.5 %copy-start.1 = (f32[64]{0:T(128)S(1)}, f32[64]{0:T(128)}, u32[]{:S(2)}) copy-start(f32[64]{0:T(128)} %param.326) | copy-start | bytes 772
  87.1 36.4 %all-to-all-start.10 = ((f32[4,64,256]{2,1,0:T(8,128)}), f32[4,64,256]{2,1,0:T(8,128)S(1)}, u32[]{:S(2)}, u32[]{:S(2)}) async-start(f32[4,64,256]{2,1,0:T(8,128)} %get-tuple-element.912), calls=%async_computation.10 | async-start | bytes 524288 | tf_op jit(solution)/shard_map/all_to_all | solution.py:185
  92.7 29.3 %collective-permute-start.229 = (bf16[64,256]{1,0:T(8,128)(2,1)S(1)}, bf16[64,256]{1,0:T(8,128)(2,1)}, u32[]{:S(2)}, u32[]{:S(2)}) collective-permute-start(bf16[64,256]{1,0:T(8,128)(2,1)S(1)} %get-tuple-element.869), channel_id=1, source_target_pairs={{81,0},{80,1},{83,2},{82,3},{85,4},{84,5},{87,6},{86,7},{89,8},{88... | collective-permute-start | bytes 98312 | tf_op jit(solution)/shard_map/cond/branch_4_fun/ppermute | solution.py:67
  108.0 13.9 %collective-permute-start.218 = (bf16[64,256]{1,0:T(8,128)(2,1)S(1)}, bf16[64,256]{1,0:T(8,128)(2,1)}, u32[]{:S(2)}, u32[]{:S(2)}) collective-permute-start(bf16[64,256]{1,0:T(8,128)(2,1)S(1)} %param.238), channel_id=1, source_target_pairs={{49,0},{48,1},{51,2},{50,3},{53,4},{52,5},{55,6},{54,7},{57,8},{56... | collective-permute-start | bytes 98312 | tf_op jit(solution)/shard_map/cond/branch_4_fun/cond/branch_2_fun/ppermute | solution.py:67
  123.6 12.0 %all-to-all-start.11 = ((bf16[8,64,256]{2,1,0:T(8,128)(2,1)}), bf16[8,64,256]{2,1,0:T(8,128)(2,1)S(1)}, u32[]{:S(2)}, u32[]{:S(2)}) async-start(bf16[8,64,256]{2,1,0:T(8,128)(2,1)} %select_add_fusion), calls=%async_computation.11 | async-start | bytes 524288 | tf_op jit(solution)/shard_map/all_to_all | solution.py:185
where the time goes:
time: 137 us; the launch traced here: 136 us
  starting transfers between devices  70.3 us (51%)
  waiting for transfers between devices  46 us (34%)
  Pallas kernels  9.02 us (7%)
  local copies, waits for them, and re-layouts  3.84 us (3%)
  between operations  2.65 us (2%)
  other arithmetic  2.35 us (2%)
  loops' own time  2.18 us (2%)
    ppermute x5, starting transfers between devices, moved(): return lax.ppermute(value, AXES, pairs)  56.1 us
    ppermute x5, waiting for transfers between devices, moved(): return lax.ppermute(value, AXES, pairs)  39.5 us
    all_to_all x3, starting transfers between devices, exchanged(): return lax.all_to_all(value, axis, 0, 0, axis_index_groups=groups)  14.2 us
    all_to_all x3, waiting for transfers between devices, exchanged(): return lax.all_to_all(value, axis, 0, 0, axis_index_groups=groups)  6.51 us
    pallas_call x1, Pallas kernels, tiles(): pl.pallas_call(tiles_kernel, out_shape=(jax.ShapeDtypeStruct((ROUNDS, rhs...  4.95 us
    pallas_call x1, Pallas kernels, start(): pl.pallas_call(start_kernel, out_shape=(jax.ShapeDtypeStruct((desc.shape[...  4.06 us
    cond x2, local copies, waits for them, and re-layouts  3.83 us
  transfers between devices with their start and end apart: 8, of which 5 were waited for; matrix products, arithmetic and copies ran while one was open for 4% of the time, Pallas kernels for 0%

commit v1 on v0

--- a/solution.py
+++ b/solution.py
@@ -71,7 +71,7 @@
     return moved(value, side_pairs(side)) if side else value
 
 
-def start_kernel(partner, desc, dirs, packed, copies, far0, side0, far1, side1, back0, sem):
+def start_kernel(partner, desc, dirs, packed, copies, far0, side0, far1, side1, sem):
     rows = desc.shape[0]
     copy = pltpu.make_async_copy(desc, packed.at[0:rows], sem.at[0])
     copy.start()
@@ -81,7 +81,6 @@
         other = jnp.where((mask & 1) == 1, 7, jnp.where((mask & 16) == 16, 8, 9))
         far[0, 0] = jnp.where(low > 0, low - 1, other)
         side[0, 0] = ((mask >> 4) << 1) | (mask & 1)
-    back0[0, 0] = far0[0, 0] + jnp.where(far0[0, 0] < 7, 0, 3)
     for j in range(4):
         packed[rows : rows + 16, j * rows : (j + 1) * rows] = dirs[16 * j : 16 * j + 16, :]
     copy.wait()
@@ -102,9 +101,9 @@
             jax.ShapeDtypeStruct((desc.shape[0] + 16, DESC), desc.dtype),
             jax.ShapeDtypeStruct((GROUP, desc.shape[0] + 16, DESC), desc.dtype),
         )
-        + (index,) * 5,
+        + (index,) * 4,
         in_specs=[smem, pl.BlockSpec(memory_space=pl.ANY), vmem],
-        out_specs=(vmem, pl.BlockSpec(memory_space=pl.ANY)) + (smem,) * 5,
+        out_specs=(vmem, pl.BlockSpec(memory_space=pl.ANY)) + (smem,) * 4,
         scratch_shapes=[pltpu.SemaphoreType.DMA((1 + GROUP,))],
     )(partner, desc, dirs)
     return packed, copies, [step.reshape(()) for step in steps]
@@ -188,7 +187,7 @@
 def on_device(descriptors, directions, ridge, partner):
     rhs, rows = directions.shape
     weight = (ROUNDS * rows * ROW) ** (-0.5)
-    packed, copies, (far0, side0, far1, side1, back0) = start(partner, descriptors, directions)
+    packed, copies, (far0, side0, far1, side1) = start(partner, descriptors, directions)
 
     def out_first(far):
         def branch(value, side):
@@ -203,12 +202,10 @@
 
         return branch
 
-    def back_both(far):
-        def branch(first, second, other_far):
-            first = pick(
-                other_far, STEPS + 3, lambda f: lambda v: moved(v, back_pairs(f)), first
-            )
-            return first, moved(second, back_pairs(far))
+    def back_both(step):
+        def branch(first, second, other):
+            second = pick(other, STEPS, lambda f: lambda v: moved(v, back_pairs(f)), second)
+            return second, moved(first, back_pairs(step if step < 7 else step + 3))
 
         return branch
 
@@ -216,7 +213,7 @@
     group, first, second = pick(far1, STEPS, out_second, first, second, copies, side0)
     to_far, to_near = tiles(group, first, second, rhs)
     near = exchanged(to_near, "row", near_groups())
-    first, second = pick(far1, STEPS, back_both, to_far[0], to_far[1], back0)
+    second, first = pick(far0, STEPS, back_both, to_far[0], to_far[1], far1)
     env = lax.axis_index("env")
     place = (env >> 4) << 1 | (env & 1)
     slots = jnp.arange(SIDE, dtype=jnp.int32)[:, None, None]

time: 137 us -> 121 us (0.88); the launches traced: 136 us -> 119 us
  starting transfers between devices: 70.3 us -> 56.8 us
  waiting for transfers between devices: 46 us -> 43.9 us
  local copies, waits for them, and re-layouts: 3.84 us -> 1.94 us
    ppermute x5 -> x6, starting transfers between devices: 56.1 us -> 41 us  [moved(): return lax.ppermute(value, AXES, pairs)]
    ppermute x5 -> x6, waiting for transfers between devices: 39.5 us -> 37.4 us  [moved(): return lax.ppermute(value, AXES, pairs)]
    cond x2 -> x1, local copies, waits for them, and re-layouts: 3.83 us -> 1.92 us
    all_to_all x3, starting transfers between devices: 14.2 us -> 15.9 us  [exchanged(): return lax.all_to_all(value, axis, 0, 0, axis_index_groups=groups)]
  transfers between devices with their start and end apart: 8 -> 9, of which waited for: 5 -> 5; matrix products, arithmetic and copies ran while one was open for 4% -> 3% of each run, Pallas kernels for 0% -> 0%
where the time goes in v1:
time: 121 us; the launch traced here: 119 us
  starting transfers between devices  56.8 us (47%)
  waiting for transfers between devices  43.9 us (36%)
  Pallas kernels  9.09 us (8%)
  between operations  2.66 us (2%)
  other arithmetic  2.37 us (2%)
  loops' own time  2.18 us (2%)
  local copies, waits for them, and re-layouts  1.94 us (2%)
    ppermute x6, starting transfers between devices, moved(): return lax.ppermute(value, AXES, pairs)  41 us
    ppermute x6, waiting for transfers between devices, moved(): return lax.ppermute(value, AXES, pairs)  37.4 us
    all_to_all x3, starting transfers between devices, exchanged(): return lax.all_to_all(value, axis, 0, 0, axis_index_groups=groups)  15.9 us
    all_to_all x3, waiting for transfers between devices, exchanged(): return lax.all_to_all(value, axis, 0, 0, axis_index_groups=groups)  6.49 us
    pallas_call x1, Pallas kernels, tiles(): pl.pallas_call(tiles_kernel, out_shape=(jax.ShapeDtypeStruct((ROUNDS, rhs...  4.99 us
    pallas_call x1, Pallas kernels, start(): pl.pallas_call(start_kernel, out_shape=(jax.ShapeDtypeStruct((desc.shape[...  4.1 us
  transfers between devices with their start and end apart: 9, of which 5 were waited for; matrix products, arithmetic and copies ran while one was open for 3% of the time, Pallas kernels for 0%

profile of v1, /device:TPU:1, one launch (start us, length us, event | category | flops | bytes accessed | tf_op | source)
XLA Modules:
  0.0 118.9 jit_solution(9268718485065658734)
XLA Ops:
  0.0 4.1 %shard_map.46 = (bf16[272,1024]{1,0:T(8,128)(2,1)}, bf16[4,272,1024]{2,1,0:T(8,128)(2,1)}, s32[1,1]{1,0:T(1,128)}, s32[1,1]{1,0:T(1,128)}, s32[1,1]{1,0:T(1,128)}, /*index=5*/s32[1,1]{1,0:T(1,128)}) custom-call(s32[2,64]{1,0:T(2,128)} %partner.1, bf16[256,1024]{1,0:T(8,128)(2,1)} %desc.1, bf16[64,256]{1,0:T(8,128)(2,1)} %dirs.1), custom_call_target="tpu_custom_call" | custom-call | tf_op jit(solution)/shard_map/pallas_call | solution.py:98
  4.8 34.5 %conditional.33 = (bf16[272,1024]{1,0:T(8,128)(2,1)}, bf16[272,1024]{1,0:T(8,128)(2,1)}) conditional(s32[]{:T(128)} %bitcast.2, (s32[]{:T(128)}, bf16[272,1024]{1,0:T(8,128)(2,1)}) %tuple.905, (s32[]{:T(128)}, bf16[272,1024]{1,0:T(8,128)(2,1)}) %tuple.905, (s32[]{:T(128)}, bf16[272,1024]{1,0:T(8,128)(2,1)}) %tuple.905, ...), branch_computations={%region_0.0_spmd, %region_9.0_spmd, %region_18.0_spmd, %region_27.... | conditional | flops 1 | bytes 4456568 | solution.py:176
  4.8 14.9 %collective-permute-start.23 = (bf16[272,1024]{1,0:T(8,128)(2,1)}, bf16[272,1024]{1,0:T(8,128)(2,1)}, u32[]{:S(2)}, u32[]{:S(2)}) collective-permute-start(bf16[272,1024]{1,0:T(8,128)(2,1)} %get-tuple-element.740), channel_id=1, source_target_pairs={{0,49},{1,48},{2,51},{3,50},{4,53},{5,52},{6,55},{7,54},{8,57},{9,... | collective-permute-start | bytes 1671176 | tf_op jit(solution)/shard_map/cond/branch_2_fun/ppermute | solution.py:67
  20.4 18.8 %conditional.2 = (bf16[272,1024]{1,0:T(8,128)(2,1)}) conditional(s32[]{:T(128)} %clamp.69, bf16[272,1024]{1,0:T(8,128)(2,1)} %get-tuple-element.740, bf16[272,1024]{1,0:T(8,128)(2,1)} %get-tuple-element.740, bf16[272,1024]{1,0:T(8,128)(2,1)} %get-tuple-element.740, bf16[272,1024]{1,0:T(8,128)(2,1)} %get-tuple-element.740, ...), branch_computations={%region_19.0_spmd, %region_20.0_spmd, %region_21.0_spmd, %region_2... | conditional | bytes 2228272 | solution.py:176
  20.5 5.2 %collective-permute-start.22 = (bf16[272,1024]{1,0:T(8,128)(2,1)}, bf16[272,1024]{1,0:T(8,128)(2,1)}, u32[]{:S(2)}, u32[]{:S(2)}) collective-permute-start(bf16[272,1024]{1,0:T(8,128)(2,1)} %param.25), channel_id=1, source_target_pairs={{0,392},{1,393},{2,394},{3,395},{4,396},{5,397},{6,398},{7,399},{8... | collective-permute-start | bytes 1671176 | tf_op jit(solution)/shard_map/cond/branch_2_fun/cond/branch_7_fun/ppermute | solution.py:67
  25.7 13.6 %collective-permute-done.22 = bf16[272,1024]{1,0:T(8,128)(2,1)} collective-permute-done((bf16[272,1024]{1,0:T(8,128)(2,1)}, bf16[272,1024]{1,0:T(8,128)(2,1)}, u32[]{:S(2)}, u32[]{:S(2)}) %collective-permute-start.22) | collective-permute-done | bytes 557088 | tf_op jit(solution)/shard_map/cond/branch_2_fun/cond/branch_7_fun/ppermute | solution.py:67
  39.3 0.0 collective-permute-done.23
  39.9 37.3 %conditional.34 = (bf16[4,272,1024]{2,1,0:T(8,128)(2,1)}, bf16[272,1024]{1,0:T(8,128)(2,1)}, bf16[272,1024]{1,0:T(8,128)(2,1)}) conditional(s32[]{:T(128)} %clamp.100, (bf16[4,272,1024]{2,1,0:T(8,128)(2,1)}, s32[]{:T(128)}, bf16[272,1024]{1,0:T(8,128)(2,1)}, bf16[272,1024]{1,0:T(8,128)(2,1)}) %tuple.906, ...), branch_computations={%region_90.0_spmd, %region_99.0_spmd, %region_108.0_spmd, %region_... | conditional | flops 1 | bytes 12255392 | solution.py:176
  39.9 4.5 %all-to-all-start.3 = ((bf16[4,272,1024]{2,1,0:T(8,128)(2,1)}), bf16[4,272,1024]{2,1,0:T(8,128)(2,1)}, u32[]{:S(2)}, u32[]{:S(2)}) async-start(bf16[4,272,1024]{2,1,0:T(8,128)(2,1)} %get-tuple-element.767), calls=%async_computation.3 | async-start | bytes 4456448 | tf_op jit(solution)/shard_map/cond/branch_3_fun/all_to_all | solution.py:184
  44.4 8.0 %collective-permute-start.111 = (bf16[272,1024]{1,0:T(8,128)(2,1)}, bf16[272,1024]{1,0:T(8,128)(2,1)}, u32[]{:S(2)}, u32[]{:S(2)}) collective-permute-start(bf16[272,1024]{1,0:T(8,128)(2,1)} %get-tuple-element.770), channel_id=1, source_target_pairs={{0,65},{1,64},{2,67},{3,66},{4,69},{5,68},{6,71},{7,70},{8,73},{9,... | collective-permute-start | bytes 1671176 | tf_op jit(solution)/shard_map/cond/branch_3_fun/ppermute | solution.py:67
  53.1 5.7 %conditional.13 = (bf16[272,1024]{1,0:T(8,128)(2,1)}) conditional(s32[]{:T(128)} %clamp.80, bf16[272,1024]{1,0:T(8,128)(2,1)} %get-tuple-element.769, bf16[272,1024]{1,0:T(8,128)(2,1)} %get-tuple-element.769, bf16[272,1024]{1,0:T(8,128)(2,1)} %get-tuple-element.769, ...), branch_computations={%region_118.0_spmd, %region_119.0_spmd, %region_120.0_spmd, %regio... | conditional | bytes 2228272 | solution.py:176
  53.1 3.7 %collective-permute-start.104 = (bf16[272,1024]{1,0:T(8,128)(2,1)}, bf16[272,1024]{1,0:T(8,128)(2,1)}, u32[]{:S(2)}, u32[]{:S(2)}) collective-permute-start(bf16[272,1024]{1,0:T(8,128)(2,1)} %param.118), channel_id=1, source_target_pairs={{0,8},{1,9},{2,10},{3,11},{4,12},{5,13},{6,14},{7,15},{8,0},{9,1},... | collective-permute-start | bytes 1671176 | tf_op jit(solution)/shard_map/cond/branch_3_fun/cond/branch_1_fun/ppermute | solution.py:67
  56.9 1.9 %collective-permute-done.104 = bf16[272,1024]{1,0:T(8,128)(2,1)} collective-permute-done((bf16[272,1024]{1,0:T(8,128)(2,1)}, bf16[272,1024]{1,0:T(8,128)(2,1)}, u32[]{:S(2)}, u32[]{:S(2)}) %collective-permute-start.104) | collective-permute-done | bytes 557088 | tf_op jit(solution)/shard_map/cond/branch_3_fun/cond/branch_1_fun/ppermute | solution.py:67
  58.8 1.9 %copy.295 = bf16[272,1024]{1,0:T(8,128)(2,1)} copy(bf16[272,1024]{1,0:T(8,128)(2,1)} %get-tuple-element.942) | data formatting | bytes 1114112 | tf_op jit(solution)/shard_map/cond
  60.7 16.5 %collective-permute-done.111 = bf16[272,1024]{1,0:T(8,128)(2,1)} collective-permute-done((bf16[272,1024]{1,0:T(8,128)(2,1)}, bf16[272,1024]{1,0:T(8,128)(2,1)}, u32[]{:S(2)}, u32[]{:S(2)}) %collective-permute-start.111) | collective-permute-done | bytes 557088 | tf_op jit(solution)/shard_map/cond/branch_3_fun/ppermute | solution.py:67
  77.2 0.0 all-to-all-done.3
  77.2 5.0 %shard_map.47 = (bf16[2,64,256]{2,1,0:T(8,128)(2,1)S(1)}, f32[4,64,256]{2,1,0:T(8,128)}) custom-call(bf16[272,1024]{1,0:T(8,128)(2,1)} %get-tuple-element.848.first, bf16[272,1024]{1,0:T(8,128)(2,1)} %get-tuple-element.849.second, bf16[4,272,1024]{2,1,0:T(8,128)(2,1)} %get-tuple-element.850.group), custom_call_target="tpu_custom_call" | custom-call | flops 1207959552 | bytes 3145728 | tf_op jit(solution)/shard_map/pallas_call | solution.py:152
  82.2 0.0 copy-start
  82.2 0.0 copy-start.1
  82.2 4.0 %all-to-all-start.10 = ((f32[4,64,256]{2,1,0:T(8,128)}), f32[4,64,256]{2,1,0:T(8,128)S(1)}, u32[]{:S(2)}, u32[]{:S(2)}) async-start(f32[4,64,256]{2,1,0:T(8,128)} %get-tuple-element.851), calls=%async_computation.10 | async-start | bytes 524288 | tf_op jit(solution)/shard_map/all_to_all | solution.py:184
  87.5 15.1 %conditional.35 = (bf16[64,256]{1,0:T(8,128)(2,1)}, bf16[64,256]{1,0:T(8,128)(2,1)}) conditional(s32[]{:T(128)} %bitcast.2, (s32[]{:T(128)}, bf16[64,256]{1,0:T(8,128)(2,1)S(1)}, bf16[64,256]{1,0:T(8,128)(2,1)S(1)}) %tuple.907, (s32[]{:T(128)}, bf16[64,256]{1,0:T(8,128)(2,1)S(1)}, ...), branch_computations={%region_181.192_spmd, %region_192.203_spmd, %region_203.214_spmd, ... | conditional | flops 1 | bytes 262264 | solution.py:176
  87.6 5.6 %collective-permute-start.192 = (bf16[64,256]{1,0:T(8,128)(2,1)S(1)}, bf16[64,256]{1,0:T(8,128)(2,1)}, u32[]{:S(2)}, u32[]{:S(2)}) collective-permute-start(bf16[64,256]{1,0:T(8,128)(2,1)S(1)} %get-tuple-element.803), channel_id=1, source_target_pairs={{49,0},{48,1},{51,2},{50,3},{53,4},{52,5},{55,6},{54,7},{57,8},{56... | collective-permute-start | bytes 98312 | tf_op jit(solution)/shard_map/cond/branch_2_fun/ppermute | solution.py:67
  93.8 8.8 %conditional.22 = (bf16[64,256]{1,0:T(8,128)(2,1)}) conditional(s32[]{:T(128)} %clamp.89, bf16[64,256]{1,0:T(8,128)(2,1)S(1)} %get-tuple-element.802, bf16[64,256]{1,0:T(8,128)(2,1)S(1)} %get-tuple-element.802, bf16[64,256]{1,0:T(8,128)(2,1)S(1)} %get-tuple-element.802, ...), branch_computations={%region_204.0_spmd, %region_205.0_spmd, %region_206.0_spmd, %regio... | conditional | bytes 131120 | solution.py:176
  93.8 3.4 %collective-permute-start.185 = (bf16[64,256]{1,0:T(8,128)(2,1)S(1)}, bf16[64,256]{1,0:T(8,128)(2,1)}, u32[]{:S(2)}, u32[]{:S(2)}) collective-permute-start(bf16[64,256]{1,0:T(8,128)(2,1)S(1)} %param.205), channel_id=1, source_target_pairs={{65,0},{64,1},{67,2},{66,3},{69,4},{68,5},{71,6},{70,7},{73,8},{72... | collective-permute-start | bytes 98312 | tf_op jit(solution)/shard_map/cond/branch_2_fun/cond/branch_3_fun/ppermute | solution.py:67
  97.2 5.4 %collective-permute-done.185 = bf16[64,256]{1,0:T(8,128)(2,1)} collective-permute-done((bf16[64,256]{1,0:T(8,128)(2,1)S(1)}, bf16[64,256]{1,0:T(8,128)(2,1)}, u32[]{:S(2)}, u32[]{:S(2)}) %collective-permute-start.185) | collective-permute-done | bytes 32800 | tf_op jit(solution)/shard_map/cond/branch_2_fun/cond/branch_3_fun/ppermute | solution.py:67
  102.6 0.0 collective-permute-done.192
  102.6 1.6 %select_add_fusion = bf16[8,64,256]{2,1,0:T(8,128)(2,1)} fusion(pred[8]{0:T(512)(128)(4,1)S(1)} %get-tuple-element.857, pred[8]{0:T(512)(128)(4,1)S(1)} %get-tuple-element.858, bf16[64,256]{1,0:T(8,128)(2,1)} %get-tuple-element.854, bf16[64,256]{1,0:T(8,128)(2,1)} %get-tuple-element.853), kind=kLoop, calls=%fused_computation.1 | loop fusion | flops 393216 | bytes 327696 | tf_op jit(solution)/shard_map/add | solution.py:222
  104.2 0.0 all-to-all-done.10
  104.2 7.4 %all-to-all-start.11 = ((bf16[8,64,256]{2,1,0:T(8,128)(2,1)}), bf16[8,64,256]{2,1,0:T(8,128)(2,1)S(1)}, u32[]{:S(2)}, u32[]{:S(2)}) async-start(bf16[8,64,256]{2,1,0:T(8,128)(2,1)} %select_add_fusion), calls=%async_computation.11 | async-start | bytes 524288 | tf_op jit(solution)/shard_map/all_to_all | solution.py:184
  111.7 6.5 %all-to-all-done.11 = bf16[8,64,256]{2,1,0:T(8,128)(2,1)S(1)} async-done(((bf16[8,64,256]{2,1,0:T(8,128)(2,1)}), bf16[8,64,256]{2,1,0:T(8,128)(2,1)S(1)}, u32[]{:S(2)}, u32[]{:S(2)}) %all-to-all-start.11) | async-done | bytes 262176 | tf_op jit(solution)/shard_map/all_to_all | solution.py:184
  118.2 0.0 copy-done
  118.2 0.0 copy-done.1
  118.2 0.7 multiply_add_fusion
  (4 shorter events, 0.1 us)
Async XLA Ops:
  4.8 34.5 %collective-permute-start.23 = (bf16[272,1024]{1,0:T(8,128)(2,1)}, bf16[272,1024]{1,0:T(8,128)(2,1)}, u32[]{:S(2)}, u32[]{:S(2)}) collective-permute-start(bf16[272,1024]{1,0:T(8,128)(2,1)} %get-tuple-element.740), channel_id=1, source_target_pairs={{0,49},{1,48},{2,51},{3,50},{4,53},{5,52},{6,55},{7,54},{8,57},{9,... | collective-permute-start | bytes 1671176 | tf_op jit(solution)/shard_map/cond/branch_2_fun/ppermute | solution.py:67
  20.5 18.8 %collective-permute-start.22 = (bf16[272,1024]{1,0:T(8,128)(2,1)}, bf16[272,1024]{1,0:T(8,128)(2,1)}, u32[]{:S(2)}, u32[]{:S(2)}) collective-permute-start(bf16[272,1024]{1,0:T(8,128)(2,1)} %param.25), channel_id=1, source_target_pairs={{0,392},{1,393},{2,394},{3,395},{4,396},{5,397},{6,398},{7,399},{8... | collective-permute-start | bytes 1671176 | tf_op jit(solution)/shard_map/cond/branch_2_fun/cond/branch_7_fun/ppermute | solution.py:67
  39.9 37.3 %all-to-all-start.3 = ((bf16[4,272,1024]{2,1,0:T(8,128)(2,1)}), bf16[4,272,1024]{2,1,0:T(8,128)(2,1)}, u32[]{:S(2)}, u32[]{:S(2)}) async-start(bf16[4,272,1024]{2,1,0:T(8,128)(2,1)} %get-tuple-element.767), calls=%async_computation.3 | async-start | bytes 4456448 | tf_op jit(solution)/shard_map/cond/branch_3_fun/all_to_all | solution.py:184
  44.4 32.8 %collective-permute-start.111 = (bf16[272,1024]{1,0:T(8,128)(2,1)}, bf16[272,1024]{1,0:T(8,128)(2,1)}, u32[]{:S(2)}, u32[]{:S(2)}) collective-permute-start(bf16[272,1024]{1,0:T(8,128)(2,1)} %get-tuple-element.770), channel_id=1, source_target_pairs={{0,65},{1,64},{2,67},{3,66},{4,69},{5,68},{6,71},{7,70},{8,73},{9,... | collective-permute-start | bytes 1671176 | tf_op jit(solution)/shard_map/cond/branch_3_fun/ppermute | solution.py:67
  53.1 5.7 %collective-permute-start.104 = (bf16[272,1024]{1,0:T(8,128)(2,1)}, bf16[272,1024]{1,0:T(8,128)(2,1)}, u32[]{:S(2)}, u32[]{:S(2)}) collective-permute-start(bf16[272,1024]{1,0:T(8,128)(2,1)} %param.118), channel_id=1, source_target_pairs={{0,8},{1,9},{2,10},{3,11},{4,12},{5,13},{6,14},{7,15},{8,0},{9,1},... | collective-permute-start | bytes 1671176 | tf_op jit(solution)/shard_map/cond/branch_3_fun/cond/branch_1_fun/ppermute | solution.py:67
  82.2 36.0 %copy-start = (bf16[64,256]{1,0:T(8,128)(2,1)S(1)}, bf16[64,256]{1,0:T(8,128)(2,1)}, u32[]{:S(2)}) copy-start(bf16[64,256]{1,0:T(8,128)(2,1)} %dirs.1) | copy-start | bytes 98308
  82.2 36.0 %copy-start.1 = (f32[64]{0:T(128)S(1)}, f32[64]{0:T(128)}, u32[]{:S(2)}) copy-start(f32[64]{0:T(128)} %param.296) | copy-start | bytes 772
  82.2 22.0 %all-to-all-start.10 = ((f32[4,64,256]{2,1,0:T(8,128)}), f32[4,64,256]{2,1,0:T(8,128)S(1)}, u32[]{:S(2)}, u32[]{:S(2)}) async-start(f32[4,64,256]{2,1,0:T(8,128)} %get-tuple-element.851), calls=%async_computation.10 | async-start | bytes 524288 | tf_op jit(solution)/shard_map/all_to_all | solution.py:184
  87.6 15.1 %collective-permute-start.192 = (bf16[64,256]{1,0:T(8,128)(2,1)S(1)}, bf16[64,256]{1,0:T(8,128)(2,1)}, u32[]{:S(2)}, u32[]{:S(2)}) collective-permute-start(bf16[64,256]{1,0:T(8,128)(2,1)S(1)} %get-tuple-element.803), channel_id=1, source_target_pairs={{49,0},{48,1},{51,2},{50,3},{53,4},{52,5},{55,6},{54,7},{57,8},{56... | collective-permute-start | bytes 98312 | tf_op jit(solution)/shard_map/cond/branch_2_fun/ppermute | solution.py:67
  93.8 8.8 %collective-permute-start.185 = (bf16[64,256]{1,0:T(8,128)(2,1)S(1)}, bf16[64,256]{1,0:T(8,128)(2,1)}, u32[]{:S(2)}, u32[]{:S(2)}) collective-permute-start(bf16[64,256]{1,0:T(8,128)(2,1)S(1)} %param.205), channel_id=1, source_target_pairs={{65,0},{64,1},{67,2},{66,3},{69,4},{68,5},{71,6},{70,7},{73,8},{72... | collective-permute-start | bytes 98312 | tf_op jit(solution)/shard_map/cond/branch_2_fun/cond/branch_3_fun/ppermute | solution.py:67
  104.2 13.9 %all-to-all-start.11 = ((bf16[8,64,256]{2,1,0:T(8,128)(2,1)}), bf16[8,64,256]{2,1,0:T(8,128)(2,1)S(1)}, u32[]{:S(2)}, u32[]{:S(2)}) async-start(bf16[8,64,256]{2,1,0:T(8,128)(2,1)} %select_add_fusion), calls=%async_computation.11 | async-start | bytes 524288 | tf_op jit(solution)/shard_map/all_to_all | solution.py:184
